TPU v7x, 32 devices: a whole 2x2x4 slice. The times are simulated.
32 devices in a mesh: row: 4 (over x, core), col: 8 (over z, y).
Axes of the slice: x: 2, y: 2, z: 4, core: 2. Of those that a mesh axis runs over, the one named last changes fastest.
Arguments:
- vectors: float32 [8192, 512], P(('row', 'col')), may hold values from -6 to 6
- hamiltonian_blocks: float32 [192, 128, 128], P(('row', 'col')), may hold values from -0.3125 to 0.3125
- block_place: int32 [192, 3], P(('row', 'col')), may hold values from 0 to 2, as said below
- live_count: int32 [32], P(('row', 'col')), may hold values from 1 to 6, as said below
- spectrum: float32 [2], replicated, may hold values from 1.5 to 3
Outputs:
- filtered: float32 [8192, 512], P(('row', 'col'))
Inputs may be any that keep to these rules, and one draw needn't show every extreme that they name: `block_place`: each row holds a block row within a domain, a domain code from 0 to 2, and a block column within a domain. `live_count`: some domain uses all 6 slots.
All inputs are finite; a program needn't handle non-finite values.
Results may differ from a plain program's by a relative error of at most 0.0001.
Values sent between devices are 32-bit elements; how exact they have to be, the bound alone decides.
A program may use at most 64 MiB of HBM per device.

v0:
```python
import jax
import jax.numpy as jnp
from jax import lax
from jax.sharding import PartitionSpec as P

HIGHEST = lax.Precision.HIGHEST


def passed_along(array, axis, by):
    count = lax.axis_size(axis)
    return lax.ppermute(array, axis, [(i, (i + by) % count) for i in range(count)])


def spread(values, index, total_count, weights):
    table = (index[:, None] == lax.iota(jnp.int32, total_count)[None, :]).astype(
        jnp.float32
    ) * weights[:, None]
    return jnp.einsum("sk,sim->kim", table, values, precision=HIGHEST)


def forward_terms(blocks, sources):
    return jnp.einsum("sij,sjm->sim", blocks, sources, precision=HIGHEST)


def transposed_terms(blocks, sources):
    return jnp.einsum("sji,sjm->sim", blocks, sources, precision=HIGHEST)


def local(vectors, hamiltonian_blocks, block_place, live_count, spectrum):
    total_rows = vectors.shape[0]
    vec_width = vectors.shape[1]
    slot_count = hamiltonian_blocks.shape[0]
    block_size = hamiltonian_blocks.shape[1]
    panel_count = total_rows // block_size
    live_mask = (lax.iota(jnp.int32, slot_count) < live_count[0]).astype(jnp.float32)
    masked = hamiltonian_blocks * live_mask[:, None, None]
    row_index = block_place[:, 0]
    targets = block_place[:, 1]
    col_index = block_place[:, 2]
    unit_weights = jnp.ones((slot_count,), jnp.float32)

    def operate(field):
        panels = field.reshape(panel_count, block_size, vec_width)
        east_panels = passed_along(field, "col", -1).reshape(panel_count, block_size, vec_width)
        south_panels = passed_along(field, "row", -1).reshape(panel_count, block_size, vec_width)
        stacked = jnp.concatenate([panels, east_panels, south_panels], axis=0)
        sources = jnp.take(stacked, targets * panel_count + col_index, axis=0)
        result = spread(forward_terms(masked, sources), row_index, panel_count, unit_weights)
        own_panels = jnp.take(panels, row_index, axis=0)
        partials = spread(
            transposed_terms(masked, own_panels),
            targets * panel_count + col_index,
            3 * panel_count,
            unit_weights,
        )
        back_east = passed_along(
            partials[panel_count : 2 * panel_count].reshape(total_rows, vec_width), "col", 1
        )
        back_south = passed_along(
            partials[2 * panel_count :].reshape(total_rows, vec_width), "row", 1
        )
        local_sum = (result + partials[:panel_count]).reshape(total_rows, vec_width)
        return local_sum + back_east + back_south

    centre = spectrum[0]
    half_width = spectrum[1]
    first = (operate(vectors) - centre * vectors) / half_width
    return 2.0 * (operate(first) - centre * first) / half_width - vectors


def solution(mesh):
    return jax.shard_map(
        local,
        mesh=mesh,
        in_specs=(
            P(("row", "col"), None),
            P(("row", "col"), None, None),
            P(("row", "col"), None),
            P(("row", "col")),
            P(),
        ),
        out_specs=P(("row", "col"), None),
        check_vma=False,
    )
```

profile of v0, /device:TPU:24, one launch (start us, length us, event | category | flops | bytes accessed | tf_op | source)
XLA Modules:
  0.0 70.8 jit_solution(10882861733315836487)
XLA Ops:
  0.0 0.9 %collective-permute-start.1 = (f32[256,512]{1,0:T(8,128)}, f32[256,512]{1,0:T(8,128)}, u32[]{:S(2)}, u32[]{:S(2)}) collective-permute-start(f32[256,512]{1,0:T(8,128)} %param.9), channel_id=1, source_target_pairs={{0,24},{8,0},{16,8},{24,16},{1,25},{9,1},{17,9},{25,17},{2,26},{10... | collective-permute-start | bytes 1572872 | tf_op jit(solution)/shard_map/ppermute | solution.py:11
  0.9 1.4 %collective-permute-start = (f32[256,512]{1,0:T(8,128)}, f32[256,512]{1,0:T(8,128)}, u32[]{:S(2)}, u32[]{:S(2)}) collective-permute-start(f32[256,512]{1,0:T(8,128)} %param.9), channel_id=1, source_target_pairs={{0,7},{1,0},{2,1},{3,2},{4,3},{5,4},{6,5},{7,6},{8,15},{9,8},{10,9... | collective-permute-start | bytes 1572872 | tf_op jit(solution)/shard_map/ppermute | solution.py:11
  3.9 1.7 %gather_fusion.1 = f32[6,128,512]{2,1,0:T(8,128)S(1)} fusion(f32[2,128,512]{2,1,0:T(8,128)} %bitcast.51, s32[1024]{0:T(1024)S(1)} %pad_clamp_fusion), kind=kCustom, calls=%fused_computation.1.clone | custom fusion | bytes 3145752 | tf_op jit(solution)/shard_map/jit(_take)/gather | solution.py:49
  5.6 1.7 %fusion.12 = f32[6,128,512]{2,1,0:T(8,128)S(1)} fusion(f32[6,128,512]{2,1,0:T(8,128)S(1)} %gather_fusion.1, pred[6]{0:T(512)(128)(4,1)S(1)} %get-tuple-element.15, f32[6,128,128]{2,1,0:T(8,128)S(1)} %copy-done.1, f32[6]{0:T(128)S(1)} %compare_convert_fusion), kind=kOutput, calls=%fused_computation.18 | convolution fusion | flops 604471296 | bytes 3538974 | tf_op jit(solution)/shard_map/sji,sjm->sim/dot_general | solution.py:26
  7.3 1.9 %fusion.4 = f32[6,128,512]{2,0,1:T(8,128)S(1)} fusion(f32[6,128,512]{2,1,0:T(8,128)S(1)} %fusion.12, s32[6]{0:T(128)S(1)} %get-tuple-element.8), kind=kOutput, calls=%fused_computation.8 | convolution fusion | flops 28311588 | bytes 3145752 | tf_op jit(solution)/shard_map/sk,sim->kim/dot_general | solution.py:18
  10.5 0.9 %copy.7 = f32[2,128,512]{2,1,0:T(8,128)} copy(f32[2,128,512]{2,0,1:T(2,128)S(1)} %get-tuple-element.13) | data formatting | bytes 1048576 | tf_op jit(solution)/shard_map/slice | solution.py:57
  12.7 1.2 %slice_bitcast_fusion = s32[6]{0:T(128)} fusion(s32[6,3]{0,1:T(4,128)} %param.11), kind=kLoop, calls=%fused_computation.67 | loop fusion | bytes 48 | tf_op jit(solution)/shard_map/eq | solution.py:15
  14.7 2.5 %pad_maximum_fusion = f32[6,128,512]{2,1,0:T(8,128)} fusion(f32[2,128,512]{2,1,0:T(8,128)} %bitcast.6, f32[2,128,512]{2,1,0:T(8,128)} %bitcast.5, f32[2,128,512]{2,1,0:T(8,128)S(1)} %bitcast.52), kind=kLoop, calls=%fused_computation.12 | loop fusion | flops 786432 | bytes 3145728 | tf_op jit(solution)/shard_map/concatenate | solution.py:46
  17.2 3.2 %gather_fusion = f32[6,128,512]{2,1,0:T(8,128)} fusion(f32[6,128,512]{2,1,0:T(8,128)} %pad_maximum_fusion, s32[1024]{0:T(1024)S(1)} %pad_clamp_fusion.1), kind=kCustom, calls=%fused_computation.clone | custom fusion | bytes 3145752 | tf_op jit(solution)/shard_map/jit(_take)/gather | solution.py:47
  20.3 2.9 %fusion.14 = f32[6,128,512]{2,1,0:T(8,128)S(1)} fusion(f32[6,128,512]{2,1,0:T(8,128)} %gather_fusion, pred[6]{0:T(512)(128)(4,1)S(1)} %get-tuple-element.6, f32[6,128,128]{2,1,0:T(8,128)S(1)} %copy-done.1, f32[6]{0:T(128)S(1)} %compare_convert_fusion), kind=kOutput, calls=%fused_computation.20 | convolution fusion | flops 604471296 | bytes 3538974 | tf_op jit(solution)/shard_map/sij,sjm->sim/dot_general | solution.py:22
  23.3 1.9 %fusion.16 = f32[2,128,512]{2,0,1:T(2,128)S(1)} fusion(f32[6,128,512]{2,1,0:T(8,128)S(1)} %fusion.14, f32[6,128,512]{2,0,1:T(8,128)S(1)} %fusion.4, s32[6]{0:T(128)S(1)} %copy-done.6), kind=kOutput, calls=%fused_computation.22 | convolution fusion | flops 9568268 | bytes 2621464 | tf_op jit(solution)/shard_map/sk,sim->kim/dot_general | solution.py:18
  25.4 2.3 %collective-permute-done.2 = f32[256,512]{1,0:T(8,128)} collective-permute-done((f32[256,512]{1,0:T(8,128)}, f32[256,512]{1,0:T(8,128)}, u32[]{:S(2)}, u32[]{:S(2)}) %collective-permute-start.2) | collective-permute-done | bytes 524320 | tf_op jit(solution)/shard_map/ppermute | solution.py:11
  27.6 2.6 %fusion.37 = f32[256,512]{1,0:T(8,128)S(1)} fusion(f32[256,512]{1,0:T(8,128)} %collective-permute-done.3, f32[256,512]{1,0:T(8,128)} %collective-permute-done.2, f32[2,128,512]{2,1,0:T(8,128)S(1)} %copy.6, f32[256,512]{1,0:T(8,128)S(1)} %copy-done, f32[]{:T(128)} %bitcast.12, f32[]{:T(128)} %bitcast.11), kind=kLoop, calls=%fused_computation.41 | loop fusion | flops 655360 | bytes 2621448 | tf_op jit(solution)/shard_map/div | solution.py:67
  30.2 1.3 %collective-permute-start.5 = (f32[256,512]{1,0:T(8,128)S(1)}, f32[256,512]{1,0:T(8,128)}, u32[]{:S(2)}, u32[]{:S(2)}) collective-permute-start(f32[256,512]{1,0:T(8,128)S(1)} %fusion.37), channel_id=1, source_target_pairs={{0,24},{8,0},{16,8},{24,16},{1,25},{9,1},{17,9},{25,17},{2,26},{10... | collective-permute-start | bytes 1572872 | tf_op jit(solution)/shard_map/ppermute | solution.py:11
  32.7 1.7 %fusion.8 = f32[6,128,512]{2,1,0:T(8,128)S(1)} fusion(f32[6,128,512]{2,1,0:T(8,128)S(1)} %gather_fusion.3, pred[6]{0:T(512)(128)(4,1)S(1)} %copy-done.5, f32[6,128,128]{2,1,0:T(8,128)S(1)} %copy-done.1, f32[6]{0:T(128)S(1)} %compare_convert_fusion), kind=kOutput, calls=%fused_computation.14 | convolution fusion | flops 604471296 | bytes 3538974 | tf_op jit(solution)/shard_map/sji,sjm->sim/dot_general | solution.py:26
  34.3 1.9 %fusion = f32[6,128,512]{2,0,1:T(8,128)S(1)} fusion(f32[6,128,512]{2,1,0:T(8,128)S(1)} %fusion.8, s32[6]{0:T(128)S(1)} %copy-done.3), kind=kOutput, calls=%fused_computation.4 | convolution fusion | flops 28311588 | bytes 3145752 | tf_op jit(solution)/shard_map/sk,sim->kim/dot_general | solution.py:18
  36.7 0.9 %copy.10 = f32[2,128,512]{2,1,0:T(8,128)} copy(f32[2,128,512]{2,0,1:T(2,128)S(1)} %get-tuple-element.11) | data formatting | bytes 1048576 | tf_op jit(solution)/shard_map/slice | solution.py:57
  38.5 1.9 %collective-permute-start.6 = (f32[256,512]{1,0:T(8,128)}, f32[256,512]{1,0:T(8,128)}, u32[]{:S(2)}, u32[]{:S(2)}) collective-permute-start(f32[256,512]{1,0:T(8,128)} %bitcast.17), channel_id=1, source_target_pairs={{0,1},{1,2},{2,3},{3,4},{4,5},{5,6},{6,7},{7,0},{8,9},{9,10},{10,1... | collective-permute-start | bytes 1572872 | tf_op jit(solution)/shard_map/ppermute | solution.py:11
  40.4 16.3 %collective-permute-done.4 = f32[256,512]{1,0:T(8,128)} collective-permute-done((f32[256,512]{1,0:T(8,128)S(1)}, f32[256,512]{1,0:T(8,128)}, u32[]{:S(2)}, u32[]{:S(2)}) %collective-permute-start.4) | collective-permute-done | bytes 524320 | tf_op jit(solution)/shard_map/ppermute | solution.py:11
  56.7 2.5 %pad_maximum_fusion.1 = f32[6,128,512]{2,1,0:T(8,128)} fusion(f32[2,128,512]{2,1,0:T(8,128)} %bitcast.15, f32[2,128,512]{2,1,0:T(8,128)} %bitcast.14, f32[2,128,512]{2,1,0:T(8,128)S(1)} %bitcast.54), kind=kLoop, calls=%fused_computation.13 | loop fusion | flops 786432 | bytes 3145728 | tf_op jit(solution)/shard_map/concatenate | solution.py:46
  59.1 3.2 %gather_fusion.2 = f32[6,128,512]{2,1,0:T(8,128)} fusion(f32[6,128,512]{2,1,0:T(8,128)} %pad_maximum_fusion.1, s32[1024]{0:T(1024)S(1)} %pad_clamp_fusion.1), kind=kCustom, calls=%fused_computation.2.clone | custom fusion | bytes 3145752 | tf_op jit(solution)/shard_map/jit(_take)/gather | solution.py:47
  62.3 2.9 %fusion.10 = f32[6,128,512]{2,1,0:T(8,128)S(1)} fusion(f32[6,128,512]{2,1,0:T(8,128)} %gather_fusion.2, pred[6]{0:T(512)(128)(4,1)S(1)} %get-tuple-element.6, f32[6,128,128]{2,1,0:T(8,128)S(1)} %copy-done.1, f32[6]{0:T(128)S(1)} %compare_convert_fusion), kind=kOutput, calls=%fused_computation.16 | convolution fusion | flops 604471296 | bytes 3538974 | tf_op jit(solution)/shard_map/sij,sjm->sim/dot_general | solution.py:22
  65.3 1.9 %fusion.19 = f32[2,128,512]{2,0,1:T(2,128)S(1)} fusion(f32[6,128,512]{2,1,0:T(8,128)S(1)} %fusion.10, f32[6,128,512]{2,0,1:T(8,128)S(1)} %fusion, s32[6]{0:T(128)S(1)} %copy-done.7), kind=kOutput, calls=%fused_computation.23 | convolution fusion | flops 9568268 | bytes 2621464 | tf_op jit(solution)/shard_map/sk,sim->kim/dot_general | solution.py:18
  67.4 3.4 %fusion.34 = f32[256,512]{1,0:T(8,128)} fusion(f32[256,512]{1,0:T(8,128)S(1)} %copy-done, f32[256,512]{1,0:T(8,128)} %collective-permute-done.7, f32[256,512]{1,0:T(8,128)} %collective-permute-done.6, f32[2,128,512]{2,1,0:T(8,128)S(1)} %copy.9, f32[256,512]{1,0:T(8,128)S(1)} %fusion.37, f32[]{:T(128)} %bitcast.12, f32[]{:T(128)} %bitcast.11), kind=kLoop, calls=%fused_computation.37 | loop fusion | flops 917504 | bytes 3145736 | tf_op jit(solution)/shard_map/sub | solution.py:68
  (41 shorter events, 6.9 us)
Async XLA Ops:
  0.0 13.9 %collective-permute-start.1 = (f32[256,512]{1,0:T(8,128)}, f32[256,512]{1,0:T(8,128)}, u32[]{:S(2)}, u32[]{:S(2)}) collective-permute-start(f32[256,512]{1,0:T(8,128)} %param.9), channel_id=1, source_target_pairs={{0,24},{8,0},{16,8},{24,16},{1,25},{9,1},{17,9},{25,17},{2,26},{10... | collective-permute-start | bytes 1572872 | tf_op jit(solution)/shard_map/ppermute | solution.py:11
  0.9 13.7 %collective-permute-start = (f32[256,512]{1,0:T(8,128)}, f32[256,512]{1,0:T(8,128)}, u32[]{:S(2)}, u32[]{:S(2)}) collective-permute-start(f32[256,512]{1,0:T(8,128)} %param.9), channel_id=1, source_target_pairs={{0,7},{1,0},{2,1},{3,2},{4,3},{5,4},{6,5},{7,6},{8,15},{9,8},{10,9... | collective-permute-start | bytes 1572872 | tf_op jit(solution)/shard_map/ppermute | solution.py:11
  3.8 1.8 %copy-start.4 = (pred[6]{0:T(512)(128)(4,1)}, pred[6]{0:T(512)(128)(4,1)S(1)}, u32[]{:S(2)}) copy-start(pred[6]{0:T(512)(128)(4,1)S(1)} %get-tuple-element.15) | copy-start | bytes 22
  3.8 8.2 %copy-start.2 = (s32[6]{0:T(128)}, s32[6]{0:T(128)S(1)}, u32[]{:S(2)}) copy-start(s32[6]{0:T(128)S(1)} %get-tuple-element.8) | copy-start | bytes 76
  3.8 1.8 %copy-start.1 = (f32[6,128,128]{2,1,0:T(8,128)S(1)}, f32[6,128,128]{2,1,0:T(8,128)}, u32[]{:S(2)}) copy-start(f32[6,128,128]{2,1,0:T(8,128)} %param.10) | copy-start | bytes 1179652
  9.6 2.5 %copy-start.8 = (f32[2]{0:T(128)S(1)}, f32[2]{0:T(128)}, u32[]{:S(2)}) copy-start(f32[2]{0:T(128)} %param.13) | copy-start | bytes 28
  9.6 5.0 %copy-start = (f32[256,512]{1,0:T(8,128)S(1)}, f32[256,512]{1,0:T(8,128)}, u32[]{:S(2)}) copy-start(f32[256,512]{1,0:T(8,128)} %param.9) | copy-start | bytes 1572868
  10.5 14.8 %collective-permute-start.3 = (f32[256,512]{1,0:T(8,128)}, f32[256,512]{1,0:T(8,128)}, u32[]{:S(2)}, u32[]{:S(2)}) collective-permute-start(f32[256,512]{1,0:T(8,128)} %bitcast.10), channel_id=1, source_target_pairs={{0,8},{8,16},{16,24},{24,0},{1,9},{9,17},{17,25},{25,1},{2,10},{10... | collective-permute-start | bytes 1572872 | tf_op jit(solution)/shard_map/ppermute | solution.py:11
  11.4 16.2 %collective-permute-start.2 = (f32[256,512]{1,0:T(8,128)}, f32[256,512]{1,0:T(8,128)}, u32[]{:S(2)}, u32[]{:S(2)}) collective-permute-start(f32[256,512]{1,0:T(8,128)} %bitcast.9), channel_id=1, source_target_pairs={{0,1},{1,2},{2,3},{3,4},{4,5},{5,6},{6,7},{7,0},{8,9},{9,10},{10,1... | collective-permute-start | bytes 1572872 | tf_op jit(solution)/shard_map/ppermute | solution.py:11
  20.3 3.0 %copy-start.6 = (s32[6]{0:T(128)S(1)}, s32[6]{0:T(128)}, u32[]{:S(2)}) copy-start(s32[6]{0:T(128)} %slice_bitcast_fusion) | copy-start | bytes 76
  30.2 10.2 %collective-permute-start.5 = (f32[256,512]{1,0:T(8,128)S(1)}, f32[256,512]{1,0:T(8,128)}, u32[]{:S(2)}, u32[]{:S(2)}) collective-permute-start(f32[256,512]{1,0:T(8,128)S(1)} %fusion.37), channel_id=1, source_target_pairs={{0,24},{8,0},{16,8},{24,16},{1,25},{9,1},{17,9},{25,17},{2,26},{10... | collective-permute-start | bytes 1572872 | tf_op jit(solution)/shard_map/ppermute | solution.py:11
  31.5 25.2 %collective-permute-start.4 = (f32[256,512]{1,0:T(8,128)S(1)}, f32[256,512]{1,0:T(8,128)}, u32[]{:S(2)}, u32[]{:S(2)}) collective-permute-start(f32[256,512]{1,0:T(8,128)S(1)} %fusion.37), channel_id=1, source_target_pairs={{0,7},{1,0},{2,1},{3,2},{4,3},{5,4},{6,5},{7,6},{8,15},{9,8},{10,9... | collective-permute-start | bytes 1572872 | tf_op jit(solution)/shard_map/ppermute | solution.py:11
  32.0 0.7 copy-start.5
  32.7 1.7 %copy-start.3 = (s32[6]{0:T(128)S(1)}, s32[6]{0:T(128)}, u32[]{:S(2)}) copy-start(s32[6]{0:T(128)} %copy-done.2) | copy-start | bytes 76
  38.5 28.9 %collective-permute-start.7 = (f32[256,512]{1,0:T(8,128)}, f32[256,512]{1,0:T(8,128)}, u32[]{:S(2)}, u32[]{:S(2)}) collective-permute-start(f32[256,512]{1,0:T(8,128)} %bitcast.18), channel_id=1, source_target_pairs={{0,8},{8,16},{16,24},{24,0},{1,9},{9,17},{17,25},{25,1},{2,10},{10... | collective-permute-start | bytes 1572872 | tf_op jit(solution)/shard_map/ppermute | solution.py:11
  38.5 28.9 %collective-permute-start.6 = (f32[256,512]{1,0:T(8,128)}, f32[256,512]{1,0:T(8,128)}, u32[]{:S(2)}, u32[]{:S(2)}) collective-permute-start(f32[256,512]{1,0:T(8,128)} %bitcast.17), channel_id=1, source_target_pairs={{0,1},{1,2},{2,3},{3,4},{4,5},{5,6},{6,7},{7,0},{8,9},{9,10},{10,1... | collective-permute-start | bytes 1572872 | tf_op jit(solution)/shard_map/ppermute | solution.py:11
  62.3 3.0 %copy-start.7 = (s32[6]{0:T(128)S(1)}, s32[6]{0:T(128)}, u32[]{:S(2)}) copy-start(s32[6]{0:T(128)} %slice_bitcast_fusion) | copy-start | bytes 76
where the time goes:
time: 71.2 us; the launch traced here: 70.8 us
  waiting for transfers between devices  19.3 us (27%)
  matrix products  16.8 us (24%)
  local copies, waits for them, and re-layouts  15.3 us (21%)
  other arithmetic  11.8 us (17%)
  starting transfers between devices  6.68 us (9%)
  between operations  0.92 us (1%)
    ppermute x8, waiting for transfers between devices, passed_along(): lax.ppermute(array, axis, [(i, (i + by) % count) for i in range(count)])  19.3 us
    dot_general x4, matrix products, spread(): return jnp.einsum('sk,sim->kim', table, values, precision=HIGHEST)  7.59 us
    ppermute x8, starting transfers between devices, passed_along(): lax.ppermute(array, axis, [(i, (i + by) % count) for i in range(count)])  6.68 us
    gather x2, local copies, waits for them, and re-layouts, operate(): sources = jnp.take(stacked, targets * panel_count + col_index, axis=0)  6.39 us
    dot_general x2, matrix products, forward_terms(): return jnp.einsum('sij,sjm->sim', blocks, sources, precision=HIGHEST)  5.89 us
    concatenate x2, other arithmetic, operate(): stacked = jnp.concatenate([panels, east_panels, south_panels], axis=0)  4.98 us
    sub x1, other arithmetic, local(): return 2.0 * (operate(first) - centre * first) / half_width - vectors  3.42 us
    dot_general x2, matrix products, transposed_terms(): return jnp.einsum('sji,sjm->sim', blocks, sources, precision=HIGHEST)  3.3 us
  transfers between devices with their start and end apart: 8, of which 3 were waited for; matrix products, arithmetic and copies ran while one was open for 54% of the time, Pallas kernels for 0%

commit v1 on v0

v1 whole, which is shorter than its diff:
```python
import functools

import jax
import jax.numpy as jnp
from jax import lax
from jax.experimental import pallas as pl
from jax.experimental.pallas import tpu as pltpu
from jax.sharding import PartitionSpec as P


CHUNKS = 2
SYM, FWD_EAST, BACK_EAST, FWD_SOUTH, BACK_SOUTH = range(5)
MESH = pl.DeviceIdType.MESH


def split_rows(x):
    high = x.astype(jnp.bfloat16)
    low = (x - high.astype(jnp.float32)).astype(jnp.bfloat16)
    return jnp.concatenate([high, high, low], axis=0)


def split_columns(x):
    high = x.astype(jnp.bfloat16)
    low = (x - high.astype(jnp.float32)).astype(jnp.bfloat16)
    return jnp.concatenate([high, low, high], axis=1)


def product(matrix, x):
    return jnp.dot(matrix, x, preferred_element_type=jnp.float32)


def kernel(
    row_count,
    col_count,
    vec_ref,
    blocks_ref,
    place_ref,
    live_ref,
    spectrum_ref,
    out_ref,
    code,
    code_in,
    blocks_in,
    dense,
    mats,
    field,
    south,
    south_out,
    north_in,
    east,
    east_out,
    west_in,
    acc,
    send_sem,
    recv_sem,
):
    rows, width = vec_ref.shape
    slots, bs, _ = blocks_ref.shape
    panels = rows // bs
    half = width // 2
    wide = half // CHUNKS

    me_row, me_col = lax.axis_index("row"), lax.axis_index("col")
    mine = lax.rem(me_col, 2)
    other = 1 - mine
    to_partner = (me_row, me_col + 1 - 2 * mine)
    to_north = (lax.rem(me_row + row_count - 1, row_count), me_col)
    to_south = (lax.rem(me_row + 1, row_count), me_col)
    to_west = (me_row, lax.rem(me_col + col_count - 2, col_count))
    to_east = (me_row, lax.rem(me_col + 2, col_count))

    barrier = pltpu.get_barrier_semaphore()
    for device in (to_partner, to_north, to_south, to_west, to_east):
        pl.semaphore_signal(barrier, inc=1, device_id=device, device_id_type=MESH)

    live = live_ref[0]
    for s in range(slots):
        value = (place_ref[s, 0] * 3 + place_ref[s, 1]) * panels + place_ref[s, 2]
        value = jnp.where(s < live, value, -1)
        code[s : s + 1, :] = jnp.full((1, bs), value, jnp.int32).astype(jnp.float32)
    pl.semaphore_wait(barrier, 5)

    started = []

    def send(src, dst, device):
        index = len(started)
        copy = pltpu.make_async_remote_copy(
            src_ref=src,
            dst_ref=dst,
            send_sem=send_sem.at[index],
            recv_sem=recv_sem.at[index],
            device_id=device,
            device_id_type=MESH,
        )
        copy.start()
        started.append(copy)
        return copy

    def columns(which, q):
        return pl.ds(pl.multiple_of(which * half + q * wide, wide), wide)

    got_code = send(code, code_in, to_partner)
    got_blocks = send(blocks_ref, blocks_in, to_partner)
    got_field = [
        send(vec_ref.at[:, columns(other, q)], field.at[0, q, mine], to_partner) for q in range(CHUNKS)
    ]
    arrivals = [[[] for _ in range(CHUNKS)] for _ in range(2)]
    for q in range(CHUNKS):
        arrivals[0][q].append(send(vec_ref.at[:, columns(mine, q)], south.at[0, q, mine], to_north))

    def assemble(source, codes, domain):
        for t in range(3):
            for a in range(panels):
                for b in range(panels):
                    total = None
                    for s in range(slots):
                        weight = jnp.where(codes[s : s + 1, :] == float((a * 3 + t) * panels + b), 1.0, 0.0)
                        term = source[s] * weight
                        total = term if total is None else total + term
                    dense[t, a * bs : (a + 1) * bs, b * bs : (b + 1) * bs] = total
        own = dense[0]
        mats[domain, SYM] = split_columns(own + own.T)
        for t, forward, back in ((1, FWD_EAST, BACK_EAST), (2, FWD_SOUTH, BACK_SOUTH)):
            matrix = dense[t]
            mats[domain, forward] = split_columns(matrix)
            mats[domain, back] = split_columns(matrix.T)

    assemble(blocks_ref, code, mine)
    for q in range(CHUNKS):
        x = vec_ref[:, columns(mine, q)]
        field[0, q, mine] = x
        south_out[0, q, mine] = product(mats[mine, BACK_SOUTH], split_rows(x))
        arrivals[0][q].append(send(south_out.at[0, q, mine], north_in.at[0, q, mine], to_south))

    got_code.wait_recv()
    got_blocks.wait_recv()
    assemble(blocks_in, code_in, other)

    def inside(step, q):
        first, second = split_rows(field[step, q, 0]), split_rows(field[step, q, 1])
        east_out[step, q] = product(mats[1, BACK_EAST], second)
        arrivals[step][q].append(send(east_out.at[step, q], west_in.at[step, q], to_east))
        if step == 1:
            south_out[step, q, 0] = product(mats[0, BACK_SOUTH], first)
            south_out[step, q, 1] = product(mats[1, BACK_SOUTH], second)
            arrivals[step][q].append(send(south_out.at[step, q], north_in.at[step, q], to_south))
        acc[q, 0] = product(mats[0, SYM], first) + product(mats[0, FWD_EAST], second)
        acc[q, 1] = product(mats[0, BACK_EAST], first) + product(mats[1, SYM], second)

    for q in range(CHUNKS):
        got_field[q].wait_recv()
        arrivals[0][q].append(send(field.at[0, q, other], south.at[0, q, other], to_north))
        arrivals[0][q].append(send(field.at[0, q, 0], east.at[0, q], to_west))
        south_out[0, q, other] = product(mats[other, BACK_SOUTH], split_rows(field[0, q, other]))
        arrivals[0][q].append(send(south_out.at[0, q, other], north_in.at[0, q, other], to_south))
        inside(0, q)

    centre = spectrum_ref[0]
    inverse = 1.0 / spectrum_ref[1]

    def finish(step, q):
        for copy in arrivals[step][q]:
            copy.wait_recv()
        upper = acc[q, 0] + product(mats[0, FWD_SOUTH], split_rows(south[step, q, 0]))
        upper = upper + north_in[step, q, 0] + west_in[step, q]
        lower = acc[q, 1] + product(mats[1, FWD_SOUTH], split_rows(south[step, q, 1]))
        lower = lower + product(mats[1, FWD_EAST], split_rows(east[step, q])) + north_in[step, q, 1]
        return (
            (upper - centre * field[step, q, 0]) * inverse,
            (lower - centre * field[step, q, 1]) * inverse,
        )

    for q in range(CHUNKS):
        upper, lower = finish(0, q)
        field[1, q, 0] = upper
        field[1, q, 1] = lower
        arrivals[1][q].append(send(field.at[1, q], south.at[1, q], to_north))
        arrivals[1][q].append(send(field.at[1, q, 0], east.at[1, q], to_west))
        inside(1, q)

    last = []
    for q in range(CHUNKS):
        upper, lower = finish(1, q)
        field[2, q, 0] = 2.0 * upper - field[0, q, 0]
        field[2, q, 1] = 2.0 * lower - field[0, q, 1]
        last.append(send(field.at[2, q, other], out_ref.at[:, columns(mine, q)], to_partner))
        out_ref[:, columns(mine, q)] = field[2, q, mine]

    for copy in last:
        copy.wait_recv()
    for copy in started:
        copy.wait_send()


def local(row_count, col_count, vectors, blocks, place, live, spectrum):
    rows, width = vectors.shape
    slots, bs, _ = blocks.shape
    wide = width // 2 // CHUNKS
    f32 = jnp.float32
    copies = 4 + CHUNKS * (1 + 1 + 2 + 1 + 1 + 2 + 2 + 1)
    vmem = pl.BlockSpec(memory_space=pltpu.VMEM)
    smem = pl.BlockSpec(memory_space=pltpu.SMEM)
    return pl.pallas_call(
        functools.partial(kernel, row_count, col_count),
        out_shape=jax.ShapeDtypeStruct((rows, width), f32),
        in_specs=[vmem, vmem, smem, smem, smem],
        out_specs=vmem,
        scratch_shapes=[
            pltpu.VMEM((8, bs), f32),
            pltpu.VMEM((8, bs), f32),
            pltpu.VMEM((slots, bs, bs), f32),
            pltpu.VMEM((3, rows, rows), f32),
            pltpu.VMEM((2, 5, rows, 3 * rows), jnp.bfloat16),
            pltpu.VMEM((3, CHUNKS, 2, rows, wide), f32),
            pltpu.VMEM((2, CHUNKS, 2, rows, wide), f32),
            pltpu.VMEM((2, CHUNKS, 2, rows, wide), f32),
            pltpu.VMEM((2, CHUNKS, 2, rows, wide), f32),
            pltpu.VMEM((2, CHUNKS, rows, wide), f32),
            pltpu.VMEM((2, CHUNKS, rows, wide), f32),
            pltpu.VMEM((2, CHUNKS, rows, wide), f32),
            pltpu.VMEM((CHUNKS, 2, rows, wide), f32),
            pltpu.SemaphoreType.DMA((copies,)),
            pltpu.SemaphoreType.DMA((copies,)),
        ],
        compiler_params=pltpu.CompilerParams(
            collective_id=0, has_side_effects=True, vmem_limit_bytes=32 * 1024 * 1024
        ),
        name="chebyshev_pair",
    )(vectors, blocks, place, live, spectrum)


def solution(mesh):
    return jax.shard_map(
        functools.partial(local, mesh.shape["row"], mesh.shape["col"]),
        mesh=mesh,
        in_specs=(
            P(("row", "col"), None),
            P(("row", "col"), None, None),
            P(("row", "col"), None),
            P(("row", "col")),
            P(),
        ),
        out_specs=P(("row", "col"), None),
        check_vma=False,
    )
```

time: 71.2 us -> 52.8 us (0.74)
  the two profiles are of different devices: /device:TPU:24 before, /device:TPU:0 now
where the time goes in v1:
time: 52.8 us; the launch traced here: 52.6 us
  Pallas kernels  48.3 us (91%)
  local copies, waits for them, and re-layouts  3.61 us (7%)
  between operations  0.67 us (1%)
    pallas_call x1, Pallas kernels, local(): pl.pallas_call(functools.partial(kernel, row_count, col_count), out_shape...  48.3 us
    unnamed x8, local copies, waits for them, and re-layouts  3.61 us

profile of v1, /device:TPU:0, one launch (start us, length us, event | category | flops | bytes accessed | tf_op | source)
XLA Modules:
  0.0 52.6 jit_solution(10673009846479863494)
XLA Ops:
  0.7 0.0 copy-start.2
  0.7 0.8 %copy.6.place_ref = s32[6,3]{1,0:T(8,128)S(1)} copy(s32[6,3]{0,1:T(4,128)} %param.7) | data formatting | bytes 144 | tf_op args[2]
  1.4 0.0 copy-done.2
  1.4 0.0 copy-start
  1.4 1.0 %copy-done = f32[256,512]{1,0:T(8,128)S(1)} copy-done((f32[256,512]{1,0:T(8,128)S(1)}, f32[256,512]{1,0:T(8,128)}, u32[]{:S(2)}) %copy-start) | copy-done | bytes 524312
  2.5 0.0 copy-start.1
  2.5 1.0 %copy-done.1 = f32[6,128,128]{2,1,0:T(8,128)S(1)} copy-done((f32[6,128,128]{2,1,0:T(8,128)S(1)}, f32[6,128,128]{2,1,0:T(8,128)}, u32[]{:S(2)}) %copy-start.1) | copy-done | bytes 393240
  3.5 48.3 %chebyshev_pair.1 = f32[256,512]{1,0:T(8,128)S(1)} custom-call(f32[256,512]{1,0:T(8,128)S(1)} %copy-done, f32[6,128,128]{2,1,0:T(8,128)S(1)} %copy-done.1, s32[6,3]{1,0:T(8,128)S(1)} %copy.6.place_ref, s32[1]{0:T(128)S(6)} %copy.8.live_ref, f32[2]{0:T(128)S(1)} %copy-done.2), custom_call_target="tpu_custom_call" | custom-call | tf_op jit(solution)/shard_map/chebyshev_pair/pallas_call | solution.py:203
  51.8 0.8 %copy.9 = f32[256,512]{1,0:T(8,128)} copy(f32[256,512]{1,0:T(8,128)S(1)} %chebyshev_pair.1) | data formatting | bytes 1048576
Async XLA Ops:
  0.7 0.8 %copy-start.2 = (f32[2]{0:T(128)S(1)}, f32[2]{0:T(128)}, u32[]{:S(2)}) copy-start(f32[2]{0:T(128)} %spectrum_ref.1) | copy-start | bytes 28
  1.4 1.0 %copy-start = (f32[256,512]{1,0:T(8,128)S(1)}, f32[256,512]{1,0:T(8,128)}, u32[]{:S(2)}) copy-start(f32[256,512]{1,0:T(8,128)} %vec_ref.1) | copy-start | bytes 1572868
  2.5 1.0 %copy-start.1 = (f32[6,128,128]{2,1,0:T(8,128)S(1)}, f32[6,128,128]{2,1,0:T(8,128)}, u32[]{:S(2)}) copy-start(f32[6,128,128]{2,1,0:T(8,128)} %blocks_ref.1) | copy-start | bytes 1179652

commit v2 on v1

v2 whole, which is shorter than its diff:
```python
import functools

import jax
import jax.numpy as jnp
from jax import lax
from jax.experimental import pallas as pl
from jax.experimental.pallas import tpu as pltpu
from jax.sharding import PartitionSpec as P


CHUNKS = 2
SYM, FWD_EAST, BACK_EAST, FWD_SOUTH, BACK_SOUTH = range(5)
MESH = pl.DeviceIdType.MESH


def split_rows(x):
    high = x.astype(jnp.bfloat16)
    low = (x - high.astype(jnp.float32)).astype(jnp.bfloat16)
    return jnp.concatenate([high, high, low], axis=0)


def split_columns(x):
    high = x.astype(jnp.bfloat16)
    low = (x - high.astype(jnp.float32)).astype(jnp.bfloat16)
    return jnp.concatenate([high, low, high], axis=1)


def product(matrix, x):
    return jnp.dot(matrix, x, preferred_element_type=jnp.float32)


def kernel(
    row_count,
    col_count,
    vec_hbm,
    blocks_hbm,
    place_ref,
    live_ref,
    spectrum_ref,
    out_ref,
    vec_ref,
    blocks_ref,
    code,
    code_in,
    blocks_in,
    mats,
    field,
    south,
    south_out,
    north_in,
    east,
    east_out,
    west_in,
    acc,
    load_sem,
    send_sem,
    recv_sem,
):
    rows, width = vec_ref.shape
    slots, bs, _ = blocks_ref.shape
    panels = rows // bs
    half = width // 2
    wide = half // CHUNKS

    load_blocks = pltpu.make_async_copy(blocks_hbm, blocks_ref, load_sem.at[0])
    load_blocks.start()
    load_vec = pltpu.make_async_copy(vec_hbm, vec_ref, load_sem.at[1])
    load_vec.start()

    me_row, me_col = lax.axis_index("row"), lax.axis_index("col")
    mine = lax.rem(me_col, 2)
    other = 1 - mine
    to_partner = (me_row, me_col + 1 - 2 * mine)
    to_north = (lax.rem(me_row + row_count - 1, row_count), me_col)
    to_south = (lax.rem(me_row + 1, row_count), me_col)
    to_west = (me_row, lax.rem(me_col + col_count - 2, col_count))
    to_east = (me_row, lax.rem(me_col + 2, col_count))

    barrier = pltpu.get_barrier_semaphore()
    for device in (to_partner, to_north, to_south, to_west, to_east):
        pl.semaphore_signal(barrier, inc=1, device_id=device, device_id_type=MESH)

    live = live_ref[0]
    for s in range(slots):
        value = (place_ref[0, s] * 3 + place_ref[1, s]) * panels + place_ref[2, s]
        value = jnp.where(s < live, value, -1)
        code[s : s + 1, :] = jnp.full((1, bs), value, jnp.int32).astype(jnp.float32)
    pl.semaphore_wait(barrier, 5)

    made = []

    def remote(src, dst, device, reuse=None):
        index = len(made) if reuse is None else reuse
        copy = pltpu.make_async_remote_copy(
            src_ref=src,
            dst_ref=dst,
            send_sem=send_sem.at[index],
            recv_sem=recv_sem.at[index],
            device_id=device,
            device_id_type=MESH,
        )
        if reuse is None:
            made.append(copy)
        return copy

    def send(src, dst, device):
        copy = remote(src, dst, device)
        copy.start()
        return copy

    def columns(which, q):
        return pl.ds(pl.multiple_of(which * half + q * wide, wide), wide)

    def even(body):
        pl.when(mine == 0)(body)

    def odd(body):
        pl.when(mine == 1)(body)

    chunks = range(CHUNKS)
    both = range(2)

    got_field = [send(vec_hbm.at[:, columns(other, 0)], field.at[0, 0, mine], to_partner)]
    got_code = send(code, code_in, to_partner)
    got_blocks = send(blocks_hbm, blocks_in, to_partner)
    for q in chunks[1:]:
        got_field.append(send(vec_hbm.at[:, columns(other, q)], field.at[0, q, mine], to_partner))

    south_copy = [[[None] * 2 for _ in chunks] for _ in both]
    north_copy = [[[None] * 2 for _ in chunks] for _ in both]
    for step in both:
        for q in chunks:
            for i, d in enumerate((mine, other)):
                src = field.at[step, q, d]
                if step == 0 and i == 0:
                    src = vec_hbm.at[:, columns(mine, q)]
                south_copy[step][q][i] = remote(src, south.at[step, q, d], to_north)
                north_copy[step][q][i] = remote(south_out.at[step, q, d], north_in.at[step, q, d], to_south)
    east_index = len(made)
    east_copy = [[remote(field.at[step, q, 0], east.at[step, q], to_west) for q in chunks] for step in both]
    west_copy = [[remote(east_out.at[step, q], west_in.at[step, q], to_east) for q in chunks] for step in both]
    early = [
        remote(vec_hbm.at[:, columns(mine, q)], east.at[0, q], to_west, east_index + q) for q in chunks
    ]

    for q in chunks:
        even(early[q].start)
        south_copy[0][q][0].start()

    def dense(source, codes, t):
        columns_of = []
        for b in range(panels):
            parts = []
            for a in range(panels):
                total = None
                for s in range(slots):
                    weight = jnp.where(codes[s : s + 1, :] == float((a * 3 + t) * panels + b), 1.0, 0.0)
                    term = source[s] * weight
                    total = term if total is None else total + term
                parts.append(total)
            columns_of.append(jnp.concatenate(parts, axis=0))
        return jnp.concatenate(columns_of, axis=1)

    def assemble_side(source, codes, domain, t, forward, back):
        matrix = dense(source, codes, t)
        mats[domain, back] = split_columns(matrix.T)
        mats[domain, forward] = split_columns(matrix)

    def assemble_own(source, codes, domain):
        matrix = dense(source, codes, 0)
        mats[domain, SYM] = split_columns(matrix + matrix.T)

    def push_east(step, q):
        east_out[step, q] = product(mats[1, BACK_EAST], split_rows(field[step, q, 1]))
        west_copy[step][q].start()

    def push_south(step, q, i, d):
        south_out[step, q, d] = product(mats[d, BACK_SOUTH], split_rows(field[step, q, d]))
        north_copy[step][q][i].start()

    load_vec.wait()
    for q in chunks:
        field[0, q, mine] = vec_ref[:, columns(mine, q)]
    load_blocks.wait()
    assemble_side(blocks_ref, code, mine, 1, FWD_EAST, BACK_EAST)

    @odd
    def _():
        for q in chunks:
            push_east(0, q)

    assemble_side(blocks_ref, code, mine, 2, FWD_SOUTH, BACK_SOUTH)
    for q in chunks:
        push_south(0, q, 0, mine)
    assemble_own(blocks_ref, code, mine)

    got_field[0].wait_recv()
    odd(east_copy[0][0].start)
    south_copy[0][0][1].start()

    got_code.wait_recv()
    got_blocks.wait_recv()
    assemble_side(blocks_in, code_in, other, 1, FWD_EAST, BACK_EAST)

    @even
    def _():
        push_east(0, 0)

    assemble_side(blocks_in, code_in, other, 2, FWD_SOUTH, BACK_SOUTH)
    push_south(0, 0, 1, other)
    for q in chunks[1:]:
        got_field[q].wait_recv()
        odd(east_copy[0][q].start)
        south_copy[0][q][1].start()

        @even
        def _():
            push_east(0, q)

        push_south(0, q, 1, other)
    assemble_own(blocks_in, code_in, other)

    def inside(step, q):
        first, second = split_rows(field[step, q, 0]), split_rows(field[step, q, 1])
        acc[q, 0] = product(mats[0, SYM], first) + product(mats[0, FWD_EAST], second)
        acc[q, 1] = product(mats[0, BACK_EAST], first) + product(mats[1, SYM], second)

    for q in chunks:
        inside(0, q)

    centre = spectrum_ref[0]
    inverse = 1.0 / spectrum_ref[1]

    def wait_row(step, q, i):
        south_copy[step][q][i].wait_recv()
        north_copy[step][q][i].wait_recv()

    def upper(step, q):
        total = acc[q, 0] + product(mats[0, FWD_SOUTH], split_rows(south[step, q, 0]))
        total = total + north_in[step, q, 0]
        west_copy[step][q].wait_recv()
        return (total + west_in[step, q] - centre * field[step, q, 0]) * inverse

    def lower(step, q):
        total = acc[q, 1] + product(mats[1, FWD_SOUTH], split_rows(south[step, q, 1]))
        total = total + north_in[step, q, 1]
        east_copy[step][q].wait_recv()
        total = total + product(mats[1, FWD_EAST], split_rows(east[step, q]))
        return (total - centre * field[step, q, 1]) * inverse

    for q in chunks:
        wait_row(0, q, 0)
        wait_row(0, q, 1)
        field[1, q, 0] = upper(0, q)
        even(east_copy[1][q].start)
        field[1, q, 1] = lower(0, q)
        south_copy[1][q][1].start()
        push_east(1, q)
        odd(east_copy[1][q].start)
        push_south(1, q, 1, other)
        south_copy[1][q][0].start()
        push_south(1, q, 0, mine)
        inside(1, q)

    last = [remote(field.at[2, q, other], out_ref.at[:, columns(mine, q)], to_partner) for q in chunks]

    def set_upper(q):
        field[2, q, 0] = 2.0 * upper(1, q) - field[0, q, 0]

    def set_lower(q):
        field[2, q, 1] = 2.0 * lower(1, q) - field[0, q, 1]

    for q in chunks:
        wait_row(1, q, 1)
        even(functools.partial(set_lower, q))
        odd(functools.partial(set_upper, q))
        last[q].start()
        wait_row(1, q, 0)
        even(functools.partial(set_upper, q))
        odd(functools.partial(set_lower, q))
        out_ref[:, columns(mine, q)] = field[2, q, mine]

    for copy in last:
        copy.wait_recv()
    for copy in made:
        copy.wait_send()


def local(row_count, col_count, vectors, blocks, place, live, spectrum):
    rows, width = vectors.shape
    slots, bs, _ = blocks.shape
    wide = width // 2 // CHUNKS
    f32 = jnp.float32
    copies = 2 + CHUNKS * (1 + 4 + 4 + 2 + 2 + 1)
    vmem = pl.BlockSpec(memory_space=pltpu.VMEM)
    hbm = pl.BlockSpec(memory_space=pltpu.HBM)
    smem = pl.BlockSpec(memory_space=pltpu.SMEM)
    return pl.pallas_call(
        functools.partial(kernel, row_count, col_count),
        out_shape=jax.ShapeDtypeStruct((rows, width), f32),
        in_specs=[hbm, hbm, smem, smem, smem],
        out_specs=vmem,
        scratch_shapes=[
            pltpu.VMEM((rows, width), f32),
            pltpu.VMEM((slots, bs, bs), f32),
            pltpu.VMEM((8, bs), f32),
            pltpu.VMEM((8, bs), f32),
            pltpu.VMEM((slots, bs, bs), f32),
            pltpu.VMEM((2, 5, rows, 3 * rows), jnp.bfloat16),
            pltpu.VMEM((3, CHUNKS, 2, rows, wide), f32),
            pltpu.VMEM((2, CHUNKS, 2, rows, wide), f32),
            pltpu.VMEM((2, CHUNKS, 2, rows, wide), f32),
            pltpu.VMEM((2, CHUNKS, 2, rows, wide), f32),
            pltpu.VMEM((2, CHUNKS, rows, wide), f32),
            pltpu.VMEM((2, CHUNKS, rows, wide), f32),
            pltpu.VMEM((2, CHUNKS, rows, wide), f32),
            pltpu.VMEM((CHUNKS, 2, rows, wide), f32),
            pltpu.SemaphoreType.DMA((2,)),
            pltpu.SemaphoreType.DMA((copies,)),
            pltpu.SemaphoreType.DMA((copies,)),
        ],
        compiler_params=pltpu.CompilerParams(
            collective_id=0, has_side_effects=True, vmem_limit_bytes=60 * 1024 * 1024
        ),
        name="chebyshev_pair",
    )(vectors, blocks, place.T, live, spectrum)


def solution(mesh):
    return jax.shard_map(
        functools.partial(local, mesh.shape["row"], mesh.shape["col"]),
        mesh=mesh,
        in_specs=(
            P(("row", "col"), None),
            P(("row", "col"), None, None),
            P(("row", "col"), None),
            P(("row", "col")),
            P(),
        ),
        out_specs=P(("row", "col"), None),
        check_vma=False,
    )
```

time: 52.8 us -> 44.5 us (0.84)
  Pallas kernels: 48.3 us -> 41.8 us
  local copies, waits for them, and re-layouts: 3.61 us -> 1.87 us
    pallas_call x1, Pallas kernels: 48.3 us -> 41.8 us  [local(): pl.pallas_call(functools.partial(kernel, row_count, col_count), out_shape...]
    unnamed x8 -> x1, local copies, waits for them, and re-layouts: 3.61 us -> 1.87 us
where the time goes in v2:
time: 44.5 us; the launch traced here: 44.3 us
  Pallas kernels  41.8 us (94%)
  local copies, waits for them, and re-layouts  1.87 us (4%)
  between operations  0.66 us (1%)
    pallas_call x1, Pallas kernels, local(): pl.pallas_call(functools.partial(kernel, row_count, col_count), out_shape...  41.8 us
    unnamed x1, local copies, waits for them, and re-layouts  1.87 us

profile of v2, /device:TPU:0, one launch (start us, length us, event | category | flops | bytes accessed | tf_op | source)
XLA Modules:
  0.0 44.3 jit_solution(13471201099127704372)
XLA Ops:
  0.7 41.8 %chebyshev_pair.1 = f32[256,512]{1,0:T(8,128)} custom-call(f32[256,512]{1,0:T(8,128)} %vec_hbm.1, f32[6,128,128]{2,1,0:T(8,128)} %blocks_hbm.1, s32[3,6]{1,0:T(4,128)} %bitcast.1, s32[1]{0:T(128)S(6)} %copy.7.live_ref, f32[2]{0:T(128)} %spectrum_ref.1), custom_call_target="tpu_custom_call" | custom-call | tf_op jit(solution)/shard_map/chebyshev_pair/pallas_call | solution.py:298
  42.4 1.9 %copy.8 = f32[256,512]{1,0:T(8,128)} copy(f32[256,512]{1,0:T(8,128)} %chebyshev_pair.1) | data formatting | bytes 1048576

commit v3 on v2

--- a/solution.py
+++ b/solution.py
@@ -260,8 +260,10 @@
         push_south(1, q, 1, other)
         south_copy[1][q][0].start()
         push_south(1, q, 0, mine)
+    for q in chunks:
         inside(1, q)
 
+    keep = []
     last = [remote(field.at[2, q, other], out_ref.at[:, columns(mine, q)], to_partner) for q in chunks]
 
     def set_upper(q):
@@ -278,8 +280,11 @@
         wait_row(1, q, 0)
         even(functools.partial(set_upper, q))
         odd(functools.partial(set_lower, q))
-        out_ref[:, columns(mine, q)] = field[2, q, mine]
-
+        keep.append(pltpu.make_async_copy(field.at[2, q, mine], out_ref.at[:, columns(mine, q)], load_sem.at[2 + q]))
+        keep[q].start()
+
+    for copy in keep:
+        copy.wait()
     for copy in last:
         copy.wait_recv()
     for copy in made:
@@ -299,7 +304,7 @@
         functools.partial(kernel, row_count, col_count),
         out_shape=jax.ShapeDtypeStruct((rows, width), f32),
         in_specs=[hbm, hbm, smem, smem, smem],
-        out_specs=vmem,
+        out_specs=hbm,
         scratch_shapes=[
             pltpu.VMEM((rows, width), f32),
             pltpu.VMEM((slots, bs, bs), f32),
@@ -315,7 +320,7 @@
             pltpu.VMEM((2, CHUNKS, rows, wide), f32),
             pltpu.VMEM((2, CHUNKS, rows, wide), f32),
             pltpu.VMEM((CHUNKS, 2, rows, wide), f32),
-            pltpu.SemaphoreType.DMA((2,)),
+            pltpu.SemaphoreType.DMA((2 + CHUNKS,)),
             pltpu.SemaphoreType.DMA((copies,)),
             pltpu.SemaphoreType.DMA((copies,)),
         ],

time: 44.5 us -> 43.8 us (0.984)
  Pallas kernels: 41.8 us -> 41.1 us
    pallas_call x1, Pallas kernels: 41.8 us -> 41.1 us  [local(): pl.pallas_call(functools.partial(kernel, row_count, col_count), out_shape...]
where the time goes in v3:
time: 43.8 us; the launch traced here: 43.6 us
  Pallas kernels  41.1 us (94%)
  local copies, waits for them, and re-layouts  1.87 us (4%)
  between operations  0.66 us (2%)
    pallas_call x1, Pallas kernels, local(): pl.pallas_call(functools.partial(kernel, row_count, col_count), out_shape...  41.1 us
    unnamed x1, local copies, waits for them, and re-layouts  1.87 us

profile of v3, /device:TPU:0, one launch (start us, length us, event | category | flops | bytes accessed | tf_op | source)
XLA Modules:
  0.0 43.6 jit_solution(9615165269565690076)
XLA Ops:
  0.7 41.1 %chebyshev_pair.1 = f32[256,512]{1,0:T(8,128)} custom-call(f32[256,512]{1,0:T(8,128)} %vec_hbm.1, f32[6,128,128]{2,1,0:T(8,128)} %blocks_hbm.1, s32[3,6]{1,0:T(4,128)} %bitcast.1, s32[1]{0:T(128)S(6)} %copy.7.live_ref, f32[2]{0:T(128)} %spectrum_ref.1), custom_call_target="tpu_custom_call" | custom-call | tf_op jit(solution)/shard_map/chebyshev_pair/pallas_call | solution.py:303
  41.8 1.9 %copy.8 = f32[256,512]{1,0:T(8,128)} copy(f32[256,512]{1,0:T(8,128)} %chebyshev_pair.1) | data formatting | bytes 1048576

commit v4 on v3

--- a/solution.py
+++ b/solution.py
@@ -120,8 +120,8 @@
     chunks = range(CHUNKS)
     both = range(2)
 
+    got_code = send(code, code_in, to_partner)
     got_field = [send(vec_hbm.at[:, columns(other, 0)], field.at[0, 0, mine], to_partner)]
-    got_code = send(code, code_in, to_partner)
     got_blocks = send(blocks_hbm, blocks_in, to_partner)
     for q in chunks[1:]:
         got_field.append(send(vec_hbm.at[:, columns(other, q)], field.at[0, q, mine], to_partner))

time: 43.8 us -> 43.8 us (level)
  no operation moved by 1% of the time
where the time goes in v4:
time: 43.8 us; the launch traced here: 43.6 us
  Pallas kernels  41 us (94%)
  local copies, waits for them, and re-layouts  1.87 us (4%)
  between operations  0.66 us (2%)
    pallas_call x1, Pallas kernels, local(): pl.pallas_call(functools.partial(kernel, row_count, col_count), out_shape...  41 us
    unnamed x1, local copies, waits for them, and re-layouts  1.87 us

profile of v4, /device:TPU:0, one launch (start us, length us, event | category | flops | bytes accessed | tf_op | source)
XLA Modules:
  0.0 43.6 jit_solution(7167241417311699672)
XLA Ops:
  0.7 41.0 %chebyshev_pair.1 = f32[256,512]{1,0:T(8,128)} custom-call(f32[256,512]{1,0:T(8,128)} %vec_hbm.1, f32[6,128,128]{2,1,0:T(8,128)} %blocks_hbm.1, s32[3,6]{1,0:T(4,128)} %bitcast.1, s32[1]{0:T(128)S(6)} %copy.7.live_ref, f32[2]{0:T(128)} %spectrum_ref.1), custom_call_target="tpu_custom_call" | custom-call | tf_op jit(solution)/shard_map/chebyshev_pair/pallas_call | solution.py:303
  41.7 1.9 %copy.8 = f32[256,512]{1,0:T(8,128)} copy(f32[256,512]{1,0:T(8,128)} %chebyshev_pair.1) | data formatting | bytes 1048576
